TPU v7x, 256 devices: a whole 4x4x8 slice. The times are simulated.
256 devices in a mesh: stn: 64 (over z_lo, y, x), tm: 4 (over z_hi, core).
Axes of the slice: x: 4, y: 4, z: 8 (z_hi: 2, z_lo: 4; z = z_hi * 4 + z_lo), core: 2. Of those that a mesh axis runs over, the one named last changes fastest.
Arguments:
- voltages: bfloat16 [2, 8, 1024, 12288], P(None, None, 'stn', 'tm'), may hold values from -6 to 6
- filter_taps: float32 [12, 32], replicated, may hold values from -1.75 to 1.75
Outputs:
- visibilities: float32 [256, 2, 1024, 1024], P(('stn', 'tm'))
All inputs are finite; a program needn't handle non-finite values.
Results may differ from a plain program's by a relative error of at most 0.0035.
Values may be sent and summed in bfloat16 or wider, within the bound.
A program may use at most 192 MiB of HBM per device.

v0:
```python
import math

import jax
import jax.numpy as jnp
from jax import lax
from jax.sharding import PartitionSpec as P


def from_behind(shard, axis, by):
    length = lax.axis_size(axis)
    pairs = [(i, i + by) for i in range(length) if 0 <= i + by < length]
    return lax.ppermute(shard, axis, pairs)


def dft_matrix(fine_len):
    steps_k = jnp.arange(fine_len)
    angle = (
        2.0
        * math.pi
        / fine_len
        * (steps_k[:, None] * steps_k[None, :] % fine_len).astype(jnp.float32)
    )
    cosine = jnp.cos(angle)
    sine = jnp.sin(angle)
    upper = jnp.concatenate([cosine, -sine], axis=1)
    lower = jnp.concatenate([sine, cosine], axis=1)
    return jnp.concatenate([upper, lower], axis=0) / jnp.sqrt(jnp.float32(fine_len))


def spectra_of(extended, filter_taps, spec_count):
    comp_count, coarse, inputs, _ = extended.shape
    tap_count, fine_len = filter_taps.shape
    frame_len = spec_count * fine_len
    filtered = extended[..., 0:frame_len].astype(jnp.float32) * jnp.tile(filter_taps[0], spec_count)
    for tap_idx in range(1, tap_count):
        start = tap_idx * fine_len
        filtered = filtered + extended[..., start : start + frame_len].astype(
            jnp.float32
        ) * jnp.tile(filter_taps[tap_idx], spec_count)
    framed = filtered.reshape(comp_count, coarse, inputs, spec_count, fine_len)
    weights = dft_matrix(fine_len).reshape(2, fine_len, 2, fine_len)
    turned = lax.dot_general(
        weights, framed, (((0, 1), (0, 4)), ((), ())), precision=lax.Precision.HIGHEST
    )
    turned = turned.astype(jnp.bfloat16)
    return jnp.transpose(turned, (2, 1, 0, 3, 4))


def gram_block(left, right, factor):
    left_re = jnp.concatenate([left[0], left[1]], axis=-1)
    left_im = jnp.concatenate([left[1], -left[0]], axis=-1)
    right_all = jnp.concatenate([right[0], right[1]], axis=-1)
    dims = (((1,), (1,)), ((), ()))
    vis_re = lax.dot_general(left_re, right_all, dims, preferred_element_type=jnp.float32) * factor
    vis_im = lax.dot_general(left_im, right_all, dims, preferred_element_type=jnp.float32) * factor
    return (vis_re, vis_im)


def correlate(pair_data, factor):
    vis_re, vis_im = gram_block(pair_data, pair_data, factor)
    return jnp.stack([vis_re, vis_im], axis=0)


def on_device(voltages, filter_taps):
    tap_count, fine_len = filter_taps.shape
    rim_part = voltages[..., : (tap_count - 1) * fine_len]
    rim_next = from_behind(rim_part, "tm", -1)
    extended = jnp.concatenate([voltages, rim_next], axis=-1)
    spec_count = voltages.shape[-1] // fine_len
    spectra = spectra_of(extended, filter_taps, spec_count)
    coarse = spectra.shape[0]
    by_pair = spectra.reshape(coarse * fine_len, 2, spectra.shape[3], spec_count)
    factor = 1.0 / (spec_count * lax.axis_size("tm"))
    owned = lax.all_to_all(
        lax.all_to_all(by_pair, "stn", split_axis=0, concat_axis=2, tiled=True),
        "tm",
        split_axis=0,
        concat_axis=3,
        tiled=True,
    )
    return correlate(owned[0], factor)[None]


def solution(mesh):
    placed = (P(None, None, "stn", "tm"), P())
    return jax.shard_map(
        on_device,
        mesh=mesh,
        in_specs=placed,
        out_specs=P(("stn", "tm"), None, None, None),
        check_vma=False,
    )
```

profile of v0, /device:TPU:2, one launch (start us, length us, event | category | flops | bytes accessed | tf_op | source)
XLA Modules:
  0.0 166.3 jit_solution(15957936297600213412)
XLA Ops:
  0.0 0.0 copy-start
  0.0 0.0 copy-start.1
  0.0 1.8 %slice.85 = bf16[2,8,16,352]{3,2,1,0:T(8,128)(2,1)} slice(bf16[2,8,16,3072]{3,2,1,0:T(8,128)(2,1)} %param.2), slice={[0:2], [0:8], [0:16], [0:352]} | slice | bytes 360448 | tf_op jit(solution)/shard_map/slice | solution.py:66
  1.8 1.3 collective-permute-start
  3.0 0.1 fusion.19
  3.1 0.1 fusion.17
  3.2 1.5 constant_dynamic-update-slice_fusion.1
  4.8 0.1 maximum_multiply_fusion
  4.8 0.1 div.10
  4.9 0.0 copy-done.1
  5.0 0.6 slice_bitcast_fusion.11
  5.6 0.1 mul.174
  5.7 0.1 mul.201
  5.7 0.1 mul.198
  5.8 0.1 mul.195
  5.9 0.1 mul.192
  6.0 0.1 mul.189
  6.1 0.1 mul.186
  6.2 0.6 tile.91
  6.7 0.1 mul.183
  6.8 0.6 tile.89
  7.4 0.7 mul.180
  8.1 0.7 tile.87
  8.8 0.7 mul.177
  9.5 0.7 tile.107
  10.1 0.7 mul.207
  10.8 0.6 tile.105
  11.4 0.7 mul.204
  12.1 0.0 collective-permute-done
  12.1 1.0 constant_dynamic-update-slice_fusion
  13.1 0.0 copy-done
  13.1 7.2 %multiply_add_fusion = f32[2,8,16,3072]{3,2,1,0:T(8,128)} fusion(bf16[2,8,16,3072]{3,2,1,0:T(8,128)(2,1)S(1)} %copy-done, bf16[2,8,16,3424]{3,2,1,0:T(8,128)(2,1)S(1)} %constant_dynamic-update-slice_fusion, f32[3072]{0:T(1024)} %mul.207, f32[3072]{0:T(1024)} %mul.204, f32[3072]{0:T(1024)S(1)} %mul.201, f32[3072]{0:T(1024)S(1)} %mul.198, f32[3072]{0:T(1024)S(1)} %mul.195, ...), kind=kLoop, calls=%fused_computation.6 | loop fusion | flops 27525120 | bytes 22167552 | tf_op jit(solution)/shard_map/add | solution.py:37
  20.3 8.6 %reshape.32 = f32[2,8,16,96,32]{4,3,2,1,0:T(8,128)} reshape(f32[2,8,16,3072]{3,2,1,0:T(8,128)} %multiply_add_fusion) | data formatting | bytes 6291456 | tf_op jit(solution)/shard_map/reshape | solution.py:40
  28.9 16.1 %fusion.4 = bf16[8,32,2,16,96]{4,1,3,0,2:T(8,128)(2,1)S(1)} fusion(f32[2,32,2,32,1,1]{3,2,1,0,5,4:T(2,128)S(1)} %bitcast.65, f32[2,8,16,96,32]{4,3,2,1,0:T(8,128)} %reshape.32), kind=kOutput, calls=%fused_computation.7 | convolution fusion | flops 604766208 | bytes 4734976 | tf_op jit(solution)/shard_map/dot_general | solution.py:42
  45.0 0.8 copy.12
  45.8 63.0 %all_to_all.33 = bf16[256,2,16,96]{3,2,1,0:T(8,128)(2,1)S(1)} all-to-all(bf16[256,2,16,96]{3,2,1,0:T(8,128)(2,1)S(1)} %bitcast.58), channel_id=1, replica_groups=mesh['stn'=64,'tm'=4] {'stn'}, dimensions={0} | all-to-all | bytes 3145728 | tf_op jit(solution)/shard_map/all_to_all | solution.py:75
  108.8 0.4 copy.13
  109.2 2.5 %copy.14 = bf16[4,2,1024,96]{2,3,1,0:T(8,128)(2,1)} copy(bf16[4,2,1024,96]{3,2,1,0:T(8,128)(2,1)S(1)} %bitcast.57) | data formatting | bytes 3145728 | tf_op jit(solution)/shard_map/all_to_all | solution.py:75
  111.7 46.3 %all_to_all.34 = bf16[4,2,1024,96]{2,3,1,0:T(8,128)(2,1)S(1)} all-to-all(bf16[4,2,1024,96]{2,3,1,0:T(8,128)(2,1)} %copy.14), channel_id=1, replica_groups=mesh['stn'=64,'tm'=4] {'tm'}, dimensions={0} | all-to-all | bytes 3145728 | tf_op jit(solution)/shard_map/all_to_all | solution.py:74
  157.9 0.1 copy.32
  158.0 0.1 fusion.22
  158.2 0.1 bitcast_negate_fusion
  158.3 1.9 %multiply_bitcast_fusion.1 = f32[1,1024,1024]{2,1,0:T(8,128)S(1)} fusion(bf16[1024,384]{0,1:T(8,128)(2,1)S(1)} %bitcast.63, bf16[1024,384]{0,1:T(8,128)(2,1)S(1)} %bitcast.61), kind=kOutput, calls=%fused_computation.5 | convolution fusion | flops 1614807040 | bytes 5767168 | tf_op jit(solution)/shard_map/dot_general | solution.py:54
  160.2 1.9 %multiply_bitcast_fusion = f32[1,1024,1024]{2,1,0:T(8,128)S(1)} fusion(bf16[1024,384]{0,1:T(8,128)(2,1)S(1)} %bitcast_negate_fusion, bf16[1024,384]{0,1:T(8,128)(2,1)S(1)} %bitcast.64, bf16[1024,384]{0,1:T(8,128)(2,1)S(1)} %bitcast.62), kind=kOutput, calls=%fused_computation.4 | convolution fusion | flops 1617952768 | bytes 6553600 | tf_op jit(solution)/shard_map/dot_general | solution.py:55
  162.1 4.2 %maximum_bitcast_fusion = f32[1,2,1024,1024]{3,2,1,0:T(8,128)} fusion(f32[1,1024,1024]{2,1,0:T(8,128)S(1)} %multiply_bitcast_fusion, f32[1,1024,1024]{2,1,0:T(8,128)S(1)} %multiply_bitcast_fusion.1), kind=kLoop, calls=%fused_computation.2 | loop fusion | flops 2097152 | bytes 16777216 | tf_op jit(solution)/shard_map/broadcast_in_dim | solution.py:81
  (7 shorter events, 0.0 us)
Async XLA Ops:
  0.0 13.1 %copy-start = (bf16[2,8,16,3072]{3,2,1,0:T(8,128)(2,1)S(1)}, bf16[2,8,16,3072]{3,2,1,0:T(8,128)(2,1)}, u32[]{:S(2)}) copy-start(bf16[2,8,16,3072]{3,2,1,0:T(8,128)(2,1)} %param.2) | copy-start | bytes 4718596
  0.0 4.9 %copy-start.1 = (f32[12,32]{1,0:T(8,128)S(1)}, f32[12,32]{1,0:T(8,128)}, u32[]{:S(2)}) copy-start(f32[12,32]{1,0:T(8,128)} %param.3) | copy-start | bytes 4612
  1.8 10.3 %collective-permute-start = (bf16[2,8,16,352]{3,2,1,0:T(8,128)(2,1)}, bf16[2,8,16,352]{3,2,1,0:T(8,128)(2,1)}, u32[]{:S(2)}, u32[]{:S(2)}) collective-permute-start(bf16[2,8,16,352]{3,2,1,0:T(8,128)(2,1)} %slice.85), channel_id=1, source_target_pairs={{1,0},{2,1},{3,2},{5,4},{6,5},{7,6},{9,8},{10,9},{11,10},{13,12},{... | collective-permute-start | bytes 540680 | tf_op jit(solution)/shard_map/ppermute | solution.py:12
where the time goes:
time: 167 us; the launch traced here: 166 us
  blocking collectives  109 us (65%)
  local copies, waits for them, and re-layouts  24 us (14%)
  matrix products  19.8 us (12%)
  other arithmetic  11.8 us (7%)
    all_to_all x1, blocking collectives, on_device(): lax.all_to_all(by_pair, 'stn', split_axis=0, concat_axis=2, tiled=True)  63 us
    all_to_all x1, blocking collectives, on_device(): lax.all_to_all(lax.all_to_all(by_pair, 'stn', split_axis=0, concat_axis=2...  46.3 us
    dot_general x1, matrix products, spectra_of(): lax.dot_general(weights, framed, (((0, 1), (0, 4)), ((), ())), precision=...  16.1 us
    reshape x1, local copies, waits for them, and re-layouts, spectra_of(): framed = filtered.reshape(comp_count, coarse, inputs, spec_count, fine_len)  8.63 us
    add x1, other arithmetic, spectra_of(): filtered + extended[..., start:start + frame_len].astype(jnp.float32) * j...  7.18 us
    broadcast_in_dim x1, other arithmetic, on_device(): return correlate(owned[0], factor)[None]  4.24 us
  transfers between devices with their start and end apart: 1, of which 0 were waited for; matrix products, arithmetic and copies ran while one was open for 5% of the time, Pallas kernels for 0%

commit v1 on v0

v1 whole, which is shorter than its diff:
```python
import functools
import math

import jax
import jax.numpy as jnp
import numpy as np
from jax import lax
from jax.experimental import pallas as pl
from jax.experimental.pallas import tpu as pltpu
from jax.sharding import PartitionSpec as P

MESH = pl.DeviceIdType.MESH

COARSE = 8
INPUTS = 16
FINE = 32
TAPS = 12
FRAMES = 96
HALF = FINE // 2
BLOCK = 8
WINDOW = 640
BLOCKS = 2 * FRAMES // BLOCK
GROUPS = BLOCKS // 8
OWN = FRAMES * FINE
RIM = 384
ALL = 2 * OWN
K = 2 * WINDOW
CHUNK = 2 * 2 * FRAMES


def dft_columns():
    k = np.arange(FINE)[:, None]
    lane = np.arange(256)[None, :]
    out = np.zeros((2, 2, FINE, 256), np.float64)
    comp = (lane // 64) % 2
    for parity in range(2):
        fine = 2 * ((lane // 128) * 8 + (lane // 8) % 8) + parity
        angle = 2.0 * math.pi / FINE * (fine * k % FINE)
        out[parity, 0] = np.where(comp == 0, np.cos(angle), -np.sin(angle))
        out[parity, 1] = np.where(comp == 0, np.sin(angle), np.cos(angle))
    return (out / math.sqrt(FINE)).astype(np.float32)


def swap_groups(rows):
    rows = list(rows)
    lane = lax.broadcasted_iota(jnp.int32, rows[0].shape, 1)
    for bit in range(3):
        step = 8 << bit
        low = (lane // step) % 2 == 0
        for a in range(8):
            if a >> bit & 1:
                continue
            b = a | 1 << bit
            left, right = rows[a], rows[b]
            rows[a] = jnp.where(low, left, pltpu.roll(right, step, 1))
            rows[b] = jnp.where(low, pltpu.roll(left, 128 - step, 1), right)
    return rows


def exchange_kernel(
    volts, taps, dft, owned,
    vbuf, sbuf, w_hi, w_lo,
    load_sem, sib_send, sib_recv, rim_send, rim_recv, send_sem, recv_sem, own_sem, b_ready, bb_ready,
):
    s = lax.axis_index("stn")
    t = lax.axis_index("tm")
    zl = s // 16
    y = s // 4 % 4
    zh = t // 2
    c = t % 2
    sibling = (s, zh * 2 + 1 - c)
    barrier = pltpu.get_barrier_semaphore()

    def coarse_at(k):
        return (zl + k // 2) % 4 * 2 + (y // 2 + k) % 2

    def own_load(coarse):
        return pltpu.make_async_copy(
            volts.at[:, coarse],
            vbuf.at[:, coarse, :, pl.ds(pl.multiple_of(c * OWN, 128), OWN)],
            load_sem.at[coarse],
        )

    def to_sibling(coarse):
        return pltpu.make_async_remote_copy(
            volts.at[:, coarse],
            vbuf.at[:, coarse, :, pl.ds(pl.multiple_of(c * OWN, 128), OWN)],
            sib_send,
            sib_recv.at[coarse],
            device_id=sibling,
            device_id_type=MESH,
        )

    rim_at = pl.ds(ALL, RIM)

    pl.semaphore_signal(barrier, 1, device_id=sibling, device_id_type=MESH)

    @pl.when(zh == 0)
    def _():
        @pl.loop(0, 64)
        def _(i):
            pl.semaphore_signal(barrier, 1, device_id=((s + i) % 64, 2 + c), device_id_type=MESH)

    @pl.loop(0, COARSE)
    def _(k):
        own_load(coarse_at(k)).start()

    pl.semaphore_wait(barrier, 1 + 64 * zh)

    @pl.when(jnp.logical_and(zh == 1, c == 0))
    def _():
        @pl.loop(0, COARSE)
        def _(k):
            coarse = coarse_at(k)
            pltpu.make_async_remote_copy(
                volts.at[:, coarse, :, pl.ds(0, RIM)],
                vbuf.at[:, coarse, :, rim_at],
                rim_send,
                rim_recv.at[coarse],
                device_id=(s, 0),
                device_id_type=MESH,
            ).start()

    @pl.loop(0, COARSE)
    def _(k):
        to_sibling(coarse_at(k)).start()

    @pl.when(zh == 1)
    def _():
        @pl.loop(0, 64)
        def _(i):
            pl.semaphore_signal(b_ready, 1, device_id=((s + i) % 64, c), device_id_type=MESH)

        vbuf[:, :, :, rim_at] = jnp.zeros((2, COARSE, INPUTS, RIM), jnp.bfloat16)

    frame = lax.broadcasted_iota(jnp.int32, (FINE, 128), 1) % BLOCK
    spread = [jnp.broadcast_to(taps[:, i : i + 1], (FINE, 128)) for i in range(TAPS)]
    for seg in range(WINDOW // FINE):
        tap_of = jnp.zeros((FINE, 128), jnp.float32)
        for q in range(BLOCK):
            if 0 <= seg - q < TAPS:
                tap_of = jnp.where(frame == q, spread[seg - q], tap_of)
        for comp in range(2):
            for half in range(2):
                weight = tap_of * dft[c, comp, :, half * 128 : half * 128 + 128]
                high = weight.astype(jnp.bfloat16)
                at = (pl.ds(comp * WINDOW + seg * FINE, FINE), pl.ds(half * 128, 128))
                w_hi[at] = high
                w_lo[at] = (weight - high.astype(jnp.float32)).astype(jnp.bfloat16)

    def spectra(coarse, group):
        rows = []
        for j in range(8 * group, 8 * group + 8):
            at = pl.ds(j * BLOCK * FINE, WINDOW)
            rows.append(jnp.concatenate([vbuf[0, coarse, :, at], vbuf[1, coarse, :, at]], axis=1))
        left = jnp.concatenate(rows, axis=0)
        both = jnp.dot(left, w_hi[...], preferred_element_type=jnp.float32)
        both = both + jnp.dot(left, w_lo[...], preferred_element_type=jnp.float32)
        for half in range(2):
            turned = swap_groups(
                [both[16 * j : 16 * j + 16, 128 * half : 128 * half + 128] for j in range(8)]
            )
            for fine in range(8):
                sbuf[coarse, half * 8 + fine, :, pl.ds(group * 128, 128)] = turned[fine].astype(jnp.bfloat16)

    def send(coarse, place, to_zh):
        to_s = coarse * 8 + place
        mine = jnp.logical_and(to_s == s, to_zh == zh)
        source = sbuf.at[coarse, 2 * place + to_zh]

        @pl.when(jnp.logical_not(mine))
        def _():
            pltpu.make_async_remote_copy(
                source, owned.at[zh * 64 + s], send_sem, recv_sem,
                device_id=(to_s, to_zh * 2 + c), device_id_type=MESH,
            ).start()

        @pl.when(mine)
        def _():
            pltpu.make_async_copy(source, owned.at[zh * 64 + s], own_sem).start()

    @pl.loop(0, COARSE)
    def _(k):
        coarse = coarse_at(k)
        own_load(coarse).wait()
        to_sibling(coarse).wait_recv()
        spectra(coarse, 0)
        spectra(coarse, 1)

        @pl.when(zh == 1)
        def _():
            spectra(coarse, 2)

            @pl.loop(0, 8)
            def _(place):
                send(coarse, place, 0)

    @pl.when(zh == 0)
    def _():
        pl.semaphore_wait(b_ready, 64)
        pl.semaphore_signal(bb_ready, 1, device_id=(s, 2 + c), device_id_type=MESH)

        @pl.loop(0, COARSE)
        def _(k):
            coarse = coarse_at(k)
            rim_here = vbuf.at[:, coarse, :, rim_at]
            pltpu.make_async_copy(rim_here, rim_here, rim_recv.at[coarse]).wait()

            @pl.when(c == 0)
            def _():
                pltpu.make_async_remote_copy(
                    rim_here, rim_here, rim_send, rim_recv.at[coarse],
                    device_id=(s, 1), device_id_type=MESH,
                ).start()

            spectra(coarse, 2)

            @pl.loop(0, 16)
            def _(place):
                send(coarse, place // 2, place % 2)

    @pl.when(zh == 1)
    def _():
        pl.semaphore_wait(bb_ready, 1)

        @pl.loop(0, COARSE)
        def _(k):
            @pl.loop(0, 8)
            def _(place):
                send(coarse_at(k), place, 1)

    pltpu.make_async_copy(volts, volts, sib_send).wait()

    @pl.when(c == 0)
    def _():
        rim_all = vbuf.at[:, :, :, rim_at]
        pltpu.make_async_copy(rim_all, rim_all, rim_send).wait()

    pltpu.make_async_copy(sbuf.at[0, 0], sbuf.at[0, 0], own_sem).wait()
    sent = owned.at[pl.ds(0, 127)]
    pltpu.make_async_copy(sent, sent, send_sem).wait()
    pltpu.make_async_copy(sent, sent, recv_sem).wait()


def exchange(voltages, taps):
    vmem = pl.BlockSpec(memory_space=pltpu.VMEM)
    return pl.pallas_call(
        exchange_kernel,
        out_shape=jax.ShapeDtypeStruct((128, INPUTS, CHUNK), jnp.bfloat16),
        in_specs=[pl.BlockSpec(memory_space=pl.ANY), vmem, vmem],
        out_specs=vmem,
        scratch_shapes=[
            pltpu.VMEM((2, COARSE, INPUTS, ALL + RIM), jnp.bfloat16),
            pltpu.VMEM((COARSE, HALF, INPUTS, CHUNK), jnp.bfloat16),
            pltpu.VMEM((K, 256), jnp.bfloat16),
            pltpu.VMEM((K, 256), jnp.bfloat16),
            pltpu.SemaphoreType.DMA((COARSE,)),
            pltpu.SemaphoreType.DMA,
            pltpu.SemaphoreType.DMA((COARSE,)),
            pltpu.SemaphoreType.DMA,
            pltpu.SemaphoreType.DMA((COARSE,)),
            pltpu.SemaphoreType.DMA,
            pltpu.SemaphoreType.DMA,
            pltpu.SemaphoreType.DMA,
            pltpu.SemaphoreType.REGULAR,
            pltpu.SemaphoreType.REGULAR,
        ],
        compiler_params=pltpu.CompilerParams(
            collective_id=0, has_side_effects=True, vmem_limit_bytes=32 << 20
        ),
        name="exchange",
    )(voltages, taps, jnp.asarray(dft_columns()))


def gram_kernel(factor, data, out):
    i = pl.program_id(0)
    rows = out.shape[1]
    re = jnp.zeros((rows, 1024), jnp.float32)
    im = jnp.zeros((rows, 1024), jnp.float32)
    lane = lax.broadcasted_iota(jnp.int32, (rows, 128), 1)
    sign = jnp.where(lane < 64, 1.0, -1.0)
    at = pl.ds(pl.multiple_of(i * rows, rows), rows)
    dims = (((1,), (1,)), ((), ()))
    for zh in range(2):
        left = data[zh, at, :]
        turned = []
        for tile in range(3):
            part = left[:, tile * 128 : tile * 128 + 128].astype(jnp.float32)
            turned.append((pltpu.roll(part, 64, 1) * sign).astype(jnp.bfloat16))
        turned = jnp.concatenate(turned, axis=1)
        right = data[zh]
        re = re + lax.dot_general(left, right, dims, preferred_element_type=jnp.float32)
        im = im + lax.dot_general(turned, right, dims, preferred_element_type=jnp.float32)
    out[0] = re * factor
    out[1] = im * factor


def gram(data, factor):
    rows = 128
    return pl.pallas_call(
        functools.partial(gram_kernel, factor),
        out_shape=jax.ShapeDtypeStruct((2, 1024, 1024), jnp.float32),
        grid=(1024 // rows,),
        in_specs=[pl.BlockSpec((2, 1024, CHUNK), lambda i: (0, 0, 0))],
        out_specs=pl.BlockSpec((2, rows, 1024), lambda i: (0, i, 0)),
        compiler_params=pltpu.CompilerParams(vmem_limit_bytes=32 << 20),
        name="gram",
    )(data)


def on_device(voltages, filter_taps):
    owned = exchange(voltages, filter_taps.T)
    return gram(owned.reshape(2, 1024, CHUNK), 1.0 / (4 * FRAMES))[None]


def solution(mesh):
    return jax.shard_map(
        on_device,
        mesh=mesh,
        in_specs=(P(None, None, "stn", "tm"), P()),
        out_specs=P(("stn", "tm"), None, None, None),
        check_vma=False,
    )
```

time: 167 us -> 69 us (0.41)
  the two profiles are of different devices: /device:TPU:2 before, /device:TPU:32 now
where the time goes in v1:
time: 69 us; the launch traced here: 67.7 us
  Pallas kernels  64.6 us (94%)
  local copies, waits for them, and re-layouts  3.09 us (4%)
    pallas_call x1, Pallas kernels, exchange(): pl.pallas_call(exchange_kernel, out_shape=jax.ShapeDtypeStruct((128, INPU...  54.6 us
    pallas_call x1, Pallas kernels, gram(): pl.pallas_call(functools.partial(gram_kernel, factor), out_shape=jax.Shap...  9.98 us
    unnamed x5, local copies, waits for them, and re-layouts  3.09 us

profile of v1, /device:TPU:32, one launch (start us, length us, event | category | flops | bytes accessed | tf_op | source)
XLA Modules:
  0.0 67.7 jit_solution(17704014951547278377)
XLA Ops:
  0.0 0.8 %copy.4 = f32[12,32]{0,1:T(8,128)S(1)} copy(f32[12,32]{1,0:T(8,128)} %param.4) | data formatting | bytes 3072 | tf_op args[1]
  0.8 0.0 copy-start
  0.8 1.4 %copy-done = bf16[2,8,16,3072]{3,2,1,0:T(8,128)(2,1)S(1)} copy-done((bf16[2,8,16,3072]{3,2,1,0:T(8,128)(2,1)S(1)}, bf16[2,8,16,3072]{3,2,1,0:T(8,128)(2,1)}, u32[]{:S(2)}) %copy-start) | copy-done | bytes 1572888
  2.2 0.0 copy-start.1
  2.2 0.9 %copy-done.1 = f32[2,2,32,256]{3,2,1,0:T(8,128)S(1)} copy-done((f32[2,2,32,256]{3,2,1,0:T(8,128)S(1)}, f32[2,2,32,256]{3,2,1,0:T(8,128)}, u32[]{:S(2)}) %copy-start.1) | copy-done | bytes 131096
  3.1 54.6 %exchange.1 = bf16[128,16,384]{2,1,0:T(8,128)(2,1)S(1)} custom-call(bf16[2,8,16,3072]{3,2,1,0:T(8,128)(2,1)S(1)} %copy-done, f32[32,12]{1,0:T(8,128)S(1)} %bitcast.4, f32[2,2,32,256]{3,2,1,0:T(8,128)S(1)} %copy-done.1), custom_call_target="tpu_custom_call" | custom-call | tf_op jit(solution)/shard_map/exchange/pallas_call | solution.py:247
  57.7 10.0 %gram.1 = f32[2,1024,1024]{2,1,0:T(8,128)} custom-call(bf16[2,1024,384]{2,1,0:T(8,128)(2,1)S(1)} %bitcast.3), custom_call_target="tpu_custom_call" | custom-call | tf_op jit(solution)/shard_map/gram/pallas_call | solution.py:300
Async XLA Ops:
  0.8 1.4 %copy-start = (bf16[2,8,16,3072]{3,2,1,0:T(8,128)(2,1)S(1)}, bf16[2,8,16,3072]{3,2,1,0:T(8,128)(2,1)}, u32[]{:S(2)}) copy-start(bf16[2,8,16,3072]{3,2,1,0:T(8,128)(2,1)} %volts.1) | copy-start | bytes 4718596
  2.2 0.9 %copy-start.1 = (f32[2,2,32,256]{3,2,1,0:T(8,128)S(1)}, f32[2,2,32,256]{3,2,1,0:T(8,128)}, u32[]{:S(2)}) copy-start(f32[2,2,32,256]{3,2,1,0:T(8,128)} %constant.2.clone.dft) | copy-start | bytes 393220

commit v2 on v1

v2 whole, which is shorter than its diff:
```python
import functools
import math

import jax
import jax.numpy as jnp
from jax import lax
from jax.experimental import pallas as pl
from jax.experimental.pallas import tpu as pltpu
from jax.sharding import PartitionSpec as P

MESH = pl.DeviceIdType.MESH

COARSE = 8
INPUTS = 16
FINE = 32
TAPS = 12
FRAMES = 96
HALF = FINE // 2
BLOCK = 8
WINDOW = 640
BLOCKS = 2 * FRAMES // BLOCK
GROUPS = BLOCKS // 8
OWN = FRAMES * FINE
RIM = 384
ALL = 2 * OWN
K = 2 * WINDOW
CHUNK = 2 * 2 * FRAMES
LAG = 4
COLUMNS = 256
VMEM_LIMIT = 52 << 20


COSINES = [round(math.cos(math.pi * i / 16), 15) / math.sqrt(FINE) for i in range(17)]


def dft_columns(parity, comp, half):
    row = lax.broadcasted_iota(jnp.int32, (FINE, 128), 0)
    lane = lax.broadcasted_iota(jnp.int32, (FINE, 128), 1)
    fine = 2 * (half * 8 + lane // 8 % 8) + parity
    out = lane // 64
    turn = (fine * row + 8 * (out - comp)) & 31
    turn = jnp.minimum(turn, 32 - turn)
    value = jnp.zeros((FINE, 128), jnp.float32)
    for step in range(17):
        value = jnp.where(turn == step, COSINES[step], value)
    return value


def swap_groups(rows):
    rows = list(rows)
    lane = lax.broadcasted_iota(jnp.int32, rows[0].shape, 1)
    for bit in range(3):
        step = 8 << bit
        low = (lane // step) % 2 == 0
        for a in range(8):
            if a >> bit & 1:
                continue
            b = a | 1 << bit
            left, right = rows[a], rows[b]
            rows[a] = jnp.where(low, left, pltpu.roll(right, step, 1))
            rows[b] = jnp.where(low, pltpu.roll(left, 128 - step, 1), right)
    return rows


def exchange_kernel(
    volts, taps, owned,
    vbuf, sbuf, w_hi, w_lo,
    load_sem, sib_send, sib_recv, rim_send, rim_recv, send_sem, recv_sem, own_sem, b_ready, bb_ready,
):
    s = lax.axis_index("stn")
    t = lax.axis_index("tm")
    zl = s // 16
    y = s // 4 % 4
    zh = t // 2
    c = t % 2
    sibling = (s, zh * 2 + 1 - c)
    barrier = pltpu.get_barrier_semaphore()

    def coarse_at(k):
        return (zl + k // 2) % 4 * 2 + (y // 2 + k) % 2

    def own_load(coarse):
        return pltpu.make_async_copy(
            volts.at[:, coarse],
            vbuf.at[:, coarse, :, pl.ds(pl.multiple_of(c * OWN, 128), OWN)],
            load_sem.at[coarse],
        )

    def to_sibling(coarse):
        return pltpu.make_async_remote_copy(
            volts.at[:, coarse],
            vbuf.at[:, coarse, :, pl.ds(pl.multiple_of(c * OWN, 128), OWN)],
            sib_send,
            sib_recv.at[coarse],
            device_id=sibling,
            device_id_type=MESH,
        )

    rim_at = pl.ds(ALL, RIM)

    pl.semaphore_signal(barrier, 1, device_id=sibling, device_id_type=MESH)

    @pl.when(zh == 0)
    def _():
        @pl.loop(1, 64)
        def _(i):
            pl.semaphore_signal(barrier, 1, device_id=((s + i) % 64, c), device_id_type=MESH)

    @pl.loop(0, COARSE)
    def _(k):
        own_load(coarse_at(k)).start()

    @pl.when(zh == 0)
    def _():
        @pl.loop(0, 64)
        def _(i):
            pl.semaphore_signal(barrier, 1, device_id=((s + i) % 64, 2 + c), device_id_type=MESH)

    @pl.when(zh == 1)
    def _():
        vbuf[:, :, :, rim_at] = jnp.zeros((2, COARSE, INPUTS, RIM), jnp.bfloat16)

    eye = lax.broadcasted_iota(jnp.int32, (FINE, FINE), 0) == lax.broadcasted_iota(jnp.int32, (FINE, FINE), 1)
    turned_taps = lax.dot_general(
        eye.astype(jnp.float32), taps[...], (((1,), (1,)), ((), ())),
        precision=lax.Precision.HIGHEST, preferred_element_type=jnp.float32,
    )
    frame = lax.broadcasted_iota(jnp.int32, (FINE, 128), 1) % BLOCK
    spread = [jnp.broadcast_to(turned_taps[:, i : i + 1], (FINE, 128)) for i in range(TAPS)]
    columns = [[dft_columns(c, comp, half) for half in range(2)] for comp in range(2)]
    for seg in range(WINDOW // FINE):
        tap_of = jnp.zeros((FINE, 128), jnp.float32)
        for q in range(BLOCK):
            if 0 <= seg - q < TAPS:
                tap_of = jnp.where(frame == q, spread[seg - q], tap_of)
        for comp in range(2):
            for half in range(2):
                weight = tap_of * columns[comp][half]
                high = weight.astype(jnp.bfloat16)
                at = (pl.ds(comp * WINDOW + seg * FINE, FINE), pl.ds(half * 128, 128))
                w_hi[at] = high
                w_lo[at] = (weight - high.astype(jnp.float32)).astype(jnp.bfloat16)

    def starts(tile):
        if tile < 2:
            base = (c if tile == 0 else 1 - c) * OWN
            return [base + j * BLOCK * FINE for j in range(8)]
        return [core * OWN + j * BLOCK * FINE for core in range(2) for j in range(8, 12)]

    def spectra(coarse, tiles):
        rows = []
        for tile in tiles:
            for start in starts(tile):
                at = pl.ds(pl.multiple_of(start, 128), WINDOW)
                rows.append(jnp.concatenate([vbuf[0, coarse, :, at], vbuf[1, coarse, :, at]], axis=1))
        left = jnp.concatenate(rows, axis=0)
        both = jnp.dot(left, w_hi[...], preferred_element_type=jnp.float32)
        both = both + jnp.dot(left, w_lo[...], preferred_element_type=jnp.float32)
        for i, tile in enumerate(tiles):
            for half in range(2):
                turned = swap_groups(
                    [
                        both[16 * j : 16 * j + 16, 128 * half : 128 * half + 128]
                        for j in range(8 * i, 8 * i + 8)
                    ]
                )
                for fine in range(8):
                    sbuf[coarse, half * 8 + fine, :, pl.ds(tile * 128, 128)] = turned[fine].astype(
                        jnp.bfloat16
                    )

    def send(coarse, place, to_zh, lo, size):
        to_s = coarse * 8 + place
        mine = jnp.logical_and(to_s == s, to_zh == zh)
        part = pl.ds(lo, size)
        source = sbuf.at[coarse, 2 * place + to_zh, :, part]
        target = owned.at[zh * 64 + s, :, part]

        @pl.when(jnp.logical_not(mine))
        def _():
            pltpu.make_async_remote_copy(
                source, target, send_sem, recv_sem,
                device_id=(to_s, to_zh * 2 + c), device_id_type=MESH,
            ).start()

        @pl.when(mine)
        def _():
            pltpu.make_async_copy(source, target, own_sem).start()

    def send_first(coarse, to_zh):
        @pl.loop(0, 8)
        def _(place):
            send(coarse, place, to_zh, 0, 128)

    def start_siblings():
        @pl.loop(0, COARSE)
        def _(k):
            to_sibling(coarse_at(k)).start()

    def first(k):
        coarse = coarse_at(k)
        own_load(coarse).wait()
        spectra(coarse, (0,))

    @pl.when(zh == 0)
    def _():
        @pl.loop(0, LAG)
        def _(k):
            first(k)

    pl.semaphore_wait(barrier, 64 + zh)

    @pl.when(jnp.logical_and(zh == 1, c == 0))
    def _():
        @pl.loop(0, COARSE)
        def _(k):
            coarse = coarse_at(k)
            pltpu.make_async_remote_copy(
                volts.at[:, coarse, :, pl.ds(0, RIM)],
                vbuf.at[:, coarse, :, rim_at],
                rim_send,
                rim_recv.at[coarse],
                device_id=(s, 0),
                device_id_type=MESH,
            ).start()

    start_siblings()

    @pl.when(zh == 0)
    def _():
        @pl.loop(0, COARSE)
        def _(k):
            send_first(coarse_at(k), 0)

            @pl.when(k + LAG < COARSE)
            def _():
                first(k + LAG)

        @pl.loop(0, COARSE)
        def _(k):
            coarse = coarse_at(k)
            pl.semaphore_wait(b_ready.at[coarse], 8)
            pl.semaphore_signal(bb_ready.at[coarse], 1, device_id=(s, 2 + c), device_id_type=MESH)
            send_first(coarse, 1)

    @pl.when(zh == 1)
    def _():
        @pl.loop(0, 64)
        def _(i):
            pl.semaphore_signal(
                b_ready.at[s // 8], 1, device_id=((s + i) % 64, c), device_id_type=MESH
            )

        @pl.loop(0, COARSE)
        def _(k):
            first(k)
            send_first(coarse_at(k), 0)

        @pl.loop(0, COARSE)
        def _(k):
            coarse = coarse_at(k)
            pl.semaphore_wait(bb_ready.at[coarse], 1)
            send_first(coarse, 1)

    @pl.loop(0, COARSE)
    def _(k):
        coarse = coarse_at(k)
        to_sibling(coarse).wait_recv()

        @pl.when(zh == 0)
        def _():
            rim_here = vbuf.at[:, coarse, :, rim_at]
            pltpu.make_async_copy(rim_here, rim_here, rim_recv.at[coarse]).wait()

            @pl.when(c == 0)
            def _():
                pltpu.make_async_remote_copy(
                    rim_here, rim_here, rim_send, rim_recv.at[coarse],
                    device_id=(s, 1), device_id_type=MESH,
                ).start()

        spectra(coarse, (1, 2))

        @pl.loop(0, 16)
        def _(place):
            send(coarse, place // 2, place % 2, 128, 256)

    pltpu.make_async_copy(volts, volts, sib_send).wait()

    @pl.when(c == 0)
    def _():
        rim_all = vbuf.at[:, :, :, rim_at]
        pltpu.make_async_copy(rim_all, rim_all, rim_send).wait()

    pltpu.make_async_copy(sbuf.at[0, 0], sbuf.at[0, 0], own_sem).wait()
    sent = owned.at[pl.ds(0, 127)]
    pltpu.make_async_copy(sent, sent, send_sem).wait()
    pltpu.make_async_copy(sent, sent, recv_sem).wait()


def exchange(voltages, taps):
    vmem = pl.BlockSpec(memory_space=pltpu.VMEM)
    return pl.pallas_call(
        exchange_kernel,
        out_shape=jax.ShapeDtypeStruct((128, INPUTS, CHUNK), jnp.bfloat16),
        in_specs=[pl.BlockSpec(memory_space=pl.ANY), vmem],
        out_specs=vmem,
        scratch_shapes=[
            pltpu.VMEM((2, COARSE, INPUTS, ALL + RIM), jnp.bfloat16),
            pltpu.VMEM((COARSE, HALF, INPUTS, CHUNK), jnp.bfloat16),
            pltpu.VMEM((K, 256), jnp.bfloat16),
            pltpu.VMEM((K, 256), jnp.bfloat16),
            pltpu.SemaphoreType.DMA((COARSE,)),
            pltpu.SemaphoreType.DMA,
            pltpu.SemaphoreType.DMA((COARSE,)),
            pltpu.SemaphoreType.DMA,
            pltpu.SemaphoreType.DMA((COARSE,)),
            pltpu.SemaphoreType.DMA,
            pltpu.SemaphoreType.DMA,
            pltpu.SemaphoreType.DMA,
            pltpu.SemaphoreType.REGULAR((COARSE,)),
            pltpu.SemaphoreType.REGULAR((COARSE,)),
        ],
        compiler_params=pltpu.CompilerParams(
            collective_id=0, has_side_effects=True, vmem_limit_bytes=VMEM_LIMIT
        ),
        name="exchange",
    )(voltages, taps)


def gram_kernel(factor, data, out, buf, sems):
    lane = lax.broadcasted_iota(jnp.int32, (COLUMNS, 128), 1)
    sign = jnp.where(lane < 64, -1.0, 1.0)
    left = jnp.concatenate([data[0], data[1]], axis=1)
    copies = []
    for i in range(1024 // COLUMNS):
        at = pl.ds(i * COLUMNS, COLUMNS)
        plain, turned = [], []
        for zh in range(2):
            plain.append(data[zh, at, :])
            for tile in range(CHUNK // 128):
                part = data[zh, at, pl.ds(tile * 128, 128)].astype(jnp.float32)
                turned.append((pltpu.roll(part, 64, 1) * sign).astype(jnp.bfloat16))
        right = jnp.concatenate(
            [jnp.concatenate(plain, axis=1), jnp.concatenate(turned, axis=1)], axis=0
        )
        both = lax.dot_general(
            left, right, (((1,), (1,)), ((), ())), preferred_element_type=jnp.float32
        )
        slot = i % 2
        if i >= 2:
            copies[i - 2].wait()
        buf[slot, 0] = both[:, :COLUMNS] * factor
        buf[slot, 1] = both[:, COLUMNS:] * factor
        copies.append(pltpu.make_async_copy(buf.at[slot], out.at[:, :, at], sems.at[slot]))
        copies[i].start()
    copies[-2].wait()
    copies[-1].wait()


def gram(data, factor):
    return pl.pallas_call(
        functools.partial(gram_kernel, factor),
        out_shape=jax.ShapeDtypeStruct((2, 1024, 1024), jnp.float32),
        in_specs=[pl.BlockSpec(memory_space=pltpu.VMEM)],
        out_specs=pl.BlockSpec(memory_space=pl.ANY),
        scratch_shapes=[
            pltpu.VMEM((2, 2, 1024, COLUMNS), jnp.float32),
            pltpu.SemaphoreType.DMA((2,)),
        ],
        compiler_params=pltpu.CompilerParams(vmem_limit_bytes=48 << 20),
        name="gram",
    )(data)


def on_device(voltages, filter_taps):
    owned = exchange(voltages, filter_taps)
    return gram(owned.reshape(2, 1024, CHUNK), 1.0 / (4 * FRAMES))[None]


def solution(mesh):
    return jax.shard_map(
        on_device,
        mesh=mesh,
        in_specs=(P(None, None, "stn", "tm"), P()),
        out_specs=P(("stn", "tm"), None, None, None),
        check_vma=False,
    )
```

time: 69 us -> 61.1 us (0.89); the launches traced: 67.7 us -> 60.9 us
  Pallas kernels: 64.6 us -> 60.2 us
  local copies, waits for them, and re-layouts: 3.09 us -> 0.7 us
    pallas_call x1, Pallas kernels: 9.98 us -> 5.93 us  [gram(): pl.pallas_call(functools.partial(gram_kernel, factor), out_shape=jax.Shap...]
    unnamed x5 -> x2, local copies, waits for them, and re-layouts: 3.09 us -> 0.7 us
where the time goes in v2:
time: 61.1 us; the launch traced here: 60.9 us
  Pallas kernels  60.2 us (99%)
  local copies, waits for them, and re-layouts  0.7 us (1%)
    pallas_call x1, Pallas kernels, exchange(): pl.pallas_call(exchange_kernel, out_shape=jax.ShapeDtypeStruct((128, INPU...  54.3 us
    pallas_call x1, Pallas kernels, gram(): pl.pallas_call(functools.partial(gram_kernel, factor), out_shape=jax.Shap...  5.93 us

profile of v2, /device:TPU:32, one launch (start us, length us, event | category | flops | bytes accessed | tf_op | source)
XLA Modules:
  0.0 60.9 jit_solution(11941502743355471216)
XLA Ops:
  0.0 0.0 copy-start
  0.0 0.7 %copy-done = f32[12,32]{1,0:T(8,128)S(1)} copy-done((f32[12,32]{1,0:T(8,128)S(1)}, f32[12,32]{1,0:T(8,128)}, u32[]{:S(2)}) %copy-start) | copy-done | bytes 1560
  0.7 54.3 %exchange.1 = bf16[128,16,384]{2,1,0:T(8,128)(2,1)S(1)} custom-call(bf16[2,8,16,3072]{3,2,1,0:T(8,128)(2,1)} %volts.1, f32[12,32]{1,0:T(8,128)S(1)} %copy-done), custom_call_target="tpu_custom_call" | custom-call | tf_op jit(solution)/shard_map/exchange/pallas_call | solution.py:303
  55.0 5.9 %gram.1 = f32[2,1024,1024]{2,1,0:T(8,128)} custom-call(bf16[2,1024,384]{2,1,0:T(8,128)(2,1)S(1)} %bitcast.2), custom_call_target="tpu_custom_call" | custom-call | tf_op jit(solution)/shard_map/gram/pallas_call | solution.py:362
Async XLA Ops:
  0.0 0.7 %copy-start = (f32[12,32]{1,0:T(8,128)S(1)}, f32[12,32]{1,0:T(8,128)}, u32[]{:S(2)}) copy-start(f32[12,32]{1,0:T(8,128)} %taps.1) | copy-start | bytes 4612

commit v3 on v2

--- a/solution.py
+++ b/solution.py
@@ -25,7 +25,6 @@
 ALL = 2 * OWN
 K = 2 * WINDOW
 CHUNK = 2 * 2 * FRAMES
-LAG = 4
 COLUMNS = 256
 VMEM_LIMIT = 52 << 20
 
@@ -65,7 +64,7 @@
 def exchange_kernel(
     volts, taps, owned,
     vbuf, sbuf, w_hi, w_lo,
-    load_sem, sib_send, sib_recv, rim_send, rim_recv, send_sem, recv_sem, own_sem, b_ready, bb_ready,
+    load_sem, sib_send, sib_recv, rim_send, rim_recv, send_sem, recv_sem, own_sem, b_in, a_ready, b_ready, bb_ready,
 ):
     s = lax.axis_index("stn")
     t = lax.axis_index("tm")
@@ -74,6 +73,7 @@
     zh = t // 2
     c = t % 2
     sibling = (s, zh * 2 + 1 - c)
+    opposite = (s, 2 - 2 * zh + c)
     barrier = pltpu.get_barrier_semaphore()
 
     def coarse_at(k):
@@ -102,7 +102,9 @@
 
     @pl.when(zh == 0)
     def _():
-        @pl.loop(1, 64)
+        pl.semaphore_signal(barrier, 1, device_id=opposite, device_id_type=MESH)
+
+        @pl.loop(1, 64, unroll=9)
         def _(i):
             pl.semaphore_signal(barrier, 1, device_id=((s + i) % 64, c), device_id_type=MESH)
 
@@ -110,14 +112,31 @@
     def _(k):
         own_load(coarse_at(k)).start()
 
-    @pl.when(zh == 0)
-    def _():
-        @pl.loop(0, 64)
-        def _(i):
-            pl.semaphore_signal(barrier, 1, device_id=((s + i) % 64, 2 + c), device_id_type=MESH)
+    def start_siblings():
+        @pl.loop(0, COARSE)
+        def _(k):
+            to_sibling(coarse_at(k)).start()
 
     @pl.when(zh == 1)
     def _():
+        pl.semaphore_wait(barrier, 2)
+        pl.semaphore_signal(b_in, 1, device_id=opposite, device_id_type=MESH)
+
+        @pl.when(c == 0)
+        def _():
+            @pl.loop(0, COARSE)
+            def _(k):
+                coarse = coarse_at(k)
+                pltpu.make_async_remote_copy(
+                    volts.at[:, coarse, :, pl.ds(0, RIM)],
+                    vbuf.at[:, coarse, :, rim_at],
+                    rim_send,
+                    rim_recv.at[coarse],
+                    device_id=(s, 0),
+                    device_id_type=MESH,
+                ).start()
+
+        start_siblings()
         vbuf[:, :, :, rim_at] = jnp.zeros((2, COARSE, INPUTS, RIM), jnp.bfloat16)
 
     eye = lax.broadcasted_iota(jnp.int32, (FINE, FINE), 0) == lax.broadcasted_iota(jnp.int32, (FINE, FINE), 1)
@@ -147,27 +166,33 @@
             return [base + j * BLOCK * FINE for j in range(8)]
         return [core * OWN + j * BLOCK * FINE for core in range(2) for j in range(8, 12)]
 
-    def spectra(coarse, tiles):
+    def spectra(coarses, tiles):
         rows = []
-        for tile in tiles:
-            for start in starts(tile):
-                at = pl.ds(pl.multiple_of(start, 128), WINDOW)
-                rows.append(jnp.concatenate([vbuf[0, coarse, :, at], vbuf[1, coarse, :, at]], axis=1))
+        for coarse in coarses:
+            for tile in tiles:
+                for start in starts(tile):
+                    at = pl.ds(pl.multiple_of(start, 128), WINDOW)
+                    rows.append(
+                        jnp.concatenate([vbuf[0, coarse, :, at], vbuf[1, coarse, :, at]], axis=1)
+                    )
         left = jnp.concatenate(rows, axis=0)
         both = jnp.dot(left, w_hi[...], preferred_element_type=jnp.float32)
         both = both + jnp.dot(left, w_lo[...], preferred_element_type=jnp.float32)
-        for i, tile in enumerate(tiles):
-            for half in range(2):
-                turned = swap_groups(
-                    [
-                        both[16 * j : 16 * j + 16, 128 * half : 128 * half + 128]
-                        for j in range(8 * i, 8 * i + 8)
-                    ]
-                )
-                for fine in range(8):
-                    sbuf[coarse, half * 8 + fine, :, pl.ds(tile * 128, 128)] = turned[fine].astype(
-                        jnp.bfloat16
+        row = 0
+        for coarse in coarses:
+            for tile in tiles:
+                for half in range(2):
+                    turned = swap_groups(
+                        [
+                            both[row + 16 * j : row + 16 * j + 16, 128 * half : 128 * half + 128]
+                            for j in range(8)
+                        ]
                     )
+                    for fine in range(8):
+                        sbuf[coarse, half * 8 + fine, :, pl.ds(tile * 128, 128)] = turned[fine].astype(
+                            jnp.bfloat16
+                        )
+                row += 128
 
     def send(coarse, place, to_zh, lo, size):
         to_s = coarse * 8 + place
@@ -188,102 +213,85 @@
             pltpu.make_async_copy(source, target, own_sem).start()
 
     def send_first(coarse, to_zh):
-        @pl.loop(0, 8)
+        @pl.loop(0, 8, unroll=8)
         def _(place):
             send(coarse, place, to_zh, 0, 128)
 
-    def start_siblings():
-        @pl.loop(0, COARSE)
-        def _(k):
-            to_sibling(coarse_at(k)).start()
-
-    def first(k):
-        coarse = coarse_at(k)
-        own_load(coarse).wait()
-        spectra(coarse, (0,))
+    def first(part):
+        coarses = [coarse_at(4 * part + i) for i in range(4)]
+        for coarse in coarses:
+            own_load(coarse).wait()
+        spectra(coarses, (0,))
+
+    first(0)
 
     @pl.when(zh == 0)
     def _():
-        @pl.loop(0, LAG)
-        def _(k):
-            first(k)
-
-    pl.semaphore_wait(barrier, 64 + zh)
-
-    @pl.when(jnp.logical_and(zh == 1, c == 0))
-    def _():
-        @pl.loop(0, COARSE)
-        def _(k):
-            coarse = coarse_at(k)
-            pltpu.make_async_remote_copy(
-                volts.at[:, coarse, :, pl.ds(0, RIM)],
-                vbuf.at[:, coarse, :, rim_at],
-                rim_send,
-                rim_recv.at[coarse],
-                device_id=(s, 0),
-                device_id_type=MESH,
-            ).start()
-
-    start_siblings()
-
-    @pl.when(zh == 0)
-    def _():
-        @pl.loop(0, COARSE)
-        def _(k):
-            send_first(coarse_at(k), 0)
-
-            @pl.when(k + LAG < COARSE)
-            def _():
-                first(k + LAG)
-
-        @pl.loop(0, COARSE)
-        def _(k):
-            coarse = coarse_at(k)
-            pl.semaphore_wait(b_ready.at[coarse], 8)
-            pl.semaphore_signal(bb_ready.at[coarse], 1, device_id=(s, 2 + c), device_id_type=MESH)
-            send_first(coarse, 1)
-
-    @pl.when(zh == 1)
-    def _():
-        @pl.loop(0, 64)
+        pl.semaphore_wait(barrier, 64)
+        start_siblings()
+        pl.semaphore_wait(b_in, 1)
+        pl.semaphore_signal(a_ready, 1, device_id=opposite, device_id_type=MESH)
+        pl.semaphore_signal(b_ready.at[s // 8], 1)
+
+        @pl.loop(1, 64, unroll=9)
         def _(i):
             pl.semaphore_signal(
                 b_ready.at[s // 8], 1, device_id=((s + i) % 64, c), device_id_type=MESH
             )
 
-        @pl.loop(0, COARSE)
-        def _(k):
-            first(k)
-            send_first(coarse_at(k), 0)
-
-        @pl.loop(0, COARSE)
-        def _(k):
-            coarse = coarse_at(k)
-            pl.semaphore_wait(bb_ready.at[coarse], 1)
-            send_first(coarse, 1)
+    @pl.when(zh == 1)
+    def _():
+        pl.semaphore_wait(a_ready, 1)
+
+    @pl.loop(0, 4)
+    def _(k):
+        send_first(coarse_at(k), 0)
+
+    first(1)
+
+    @pl.loop(4, COARSE)
+    def _(k):
+        send_first(coarse_at(k), 0)
 
     @pl.loop(0, COARSE)
     def _(k):
         coarse = coarse_at(k)
-        to_sibling(coarse).wait_recv()
 
         @pl.when(zh == 0)
         def _():
-            rim_here = vbuf.at[:, coarse, :, rim_at]
-            pltpu.make_async_copy(rim_here, rim_here, rim_recv.at[coarse]).wait()
-
-            @pl.when(c == 0)
+            pl.semaphore_wait(b_ready.at[coarse], 8)
+            pl.semaphore_signal(bb_ready.at[coarse], 1, device_id=(s, 2 + c), device_id_type=MESH)
+
+        @pl.when(zh == 1)
+        def _():
+            pl.semaphore_wait(bb_ready.at[coarse], 1)
+
+        send_first(coarse, 1)
+
+    @pl.loop(0, COARSE // 2)
+    def _(pair):
+        coarses = [coarse_at(2 * pair), coarse_at(2 * pair + 1)]
+        for coarse in coarses:
+            to_sibling(coarse).wait_recv()
+
+            @pl.when(zh == 0)
             def _():
-                pltpu.make_async_remote_copy(
-                    rim_here, rim_here, rim_send, rim_recv.at[coarse],
-                    device_id=(s, 1), device_id_type=MESH,
-                ).start()
-
-        spectra(coarse, (1, 2))
-
-        @pl.loop(0, 16)
-        def _(place):
-            send(coarse, place // 2, place % 2, 128, 256)
+                rim_here = vbuf.at[:, coarse, :, rim_at]
+                pltpu.make_async_copy(rim_here, rim_here, rim_recv.at[coarse]).wait()
+
+                @pl.when(c == 0)
+                def _():
+                    pltpu.make_async_remote_copy(
+                        rim_here, rim_here, rim_send, rim_recv.at[coarse],
+                        device_id=(s, 1), device_id_type=MESH,
+                    ).start()
+
+        spectra(coarses, (1, 2))
+
+        for coarse in coarses:
+            @pl.loop(0, 16, unroll=8)
+            def _(place):
+                send(coarse, place // 2, place % 2, 128, 256)
 
     pltpu.make_async_copy(volts, volts, sib_send).wait()
 
@@ -318,6 +326,8 @@
             pltpu.SemaphoreType.DMA,
             pltpu.SemaphoreType.DMA,
             pltpu.SemaphoreType.DMA,
+            pltpu.SemaphoreType.REGULAR,
+            pltpu.SemaphoreType.REGULAR,
             pltpu.SemaphoreType.REGULAR((COARSE,)),
             pltpu.SemaphoreType.REGULAR((COARSE,)),
         ],

time: 61.1 us -> 57.6 us (0.943)
  Pallas kernels: 60.2 us -> 56.7 us
    pallas_call x1, Pallas kernels: 54.3 us -> 50.8 us  [exchange(): pl.pallas_call(exchange_kernel, out_shape=jax.ShapeDtypeStruct((128, INPU...]
where the time goes in v3:
time: 57.6 us; the launch traced here: 57.5 us
  Pallas kernels  56.7 us (98%)
  local copies, waits for them, and re-layouts  0.7 us (1%)
    pallas_call x1, Pallas kernels, exchange(): pl.pallas_call(exchange_kernel, out_shape=jax.ShapeDtypeStruct((128, INPU...  50.8 us
    pallas_call x1, Pallas kernels, gram(): pl.pallas_call(functools.partial(gram_kernel, factor), out_shape=jax.Shap...  5.94 us

profile of v3, /device:TPU:32, one launch (start us, length us, event | category | flops | bytes accessed | tf_op | source)
XLA Modules:
  0.0 57.5 jit_solution(4516652268947305056)
XLA Ops:
  0.0 0.0 copy-start
  0.0 0.7 %copy-done = f32[12,32]{1,0:T(8,128)S(1)} copy-done((f32[12,32]{1,0:T(8,128)S(1)}, f32[12,32]{1,0:T(8,128)}, u32[]{:S(2)}) %copy-start) | copy-done | bytes 1560
  0.7 50.8 %exchange.1 = bf16[128,16,384]{2,1,0:T(8,128)(2,1)S(1)} custom-call(bf16[2,8,16,3072]{3,2,1,0:T(8,128)(2,1)} %volts.1, f32[12,32]{1,0:T(8,128)S(1)} %copy-done), custom_call_target="tpu_custom_call" | custom-call | tf_op jit(solution)/shard_map/exchange/pallas_call | solution.py:311
  51.5 5.9 %gram.1 = f32[2,1024,1024]{2,1,0:T(8,128)} custom-call(bf16[2,1024,384]{2,1,0:T(8,128)(2,1)S(1)} %bitcast.2), custom_call_target="tpu_custom_call" | custom-call | tf_op jit(solution)/shard_map/gram/pallas_call | solution.py:372
Async XLA Ops:
  0.0 0.7 %copy-start = (f32[12,32]{1,0:T(8,128)S(1)}, f32[12,32]{1,0:T(8,128)}, u32[]{:S(2)}) copy-start(f32[12,32]{1,0:T(8,128)} %taps.1) | copy-start | bytes 4612

commit v4 on v3

--- a/solution.py
+++ b/solution.py
@@ -289,9 +289,17 @@
         spectra(coarses, (1, 2))
 
         for coarse in coarses:
-            @pl.loop(0, 16, unroll=8)
+            @pl.loop(0, 8, unroll=8)
             def _(place):
-                send(coarse, place // 2, place % 2, 128, 256)
+                send(coarse, place, 0, 128, 256)
+
+    @pl.loop(0, COARSE)
+    def _(k):
+        coarse = coarse_at(k)
+
+        @pl.loop(0, 8, unroll=8)
+        def _(place):
+            send(coarse, place, 1, 128, 256)
 
     pltpu.make_async_copy(volts, volts, sib_send).wait()
 
@@ -357,15 +365,12 @@
         both = lax.dot_general(
             left, right, (((1,), (1,)), ((), ())), preferred_element_type=jnp.float32
         )
-        slot = i % 2
-        if i >= 2:
-            copies[i - 2].wait()
-        buf[slot, 0] = both[:, :COLUMNS] * factor
-        buf[slot, 1] = both[:, COLUMNS:] * factor
-        copies.append(pltpu.make_async_copy(buf.at[slot], out.at[:, :, at], sems.at[slot]))
+        buf[i, 0] = both[:, :COLUMNS] * factor
+        buf[i, 1] = both[:, COLUMNS:] * factor
+        copies.append(pltpu.make_async_copy(buf.at[i], out.at[:, :, at], sems.at[i]))
         copies[i].start()
-    copies[-2].wait()
-    copies[-1].wait()
+    for copy in copies:
+        copy.wait()
 
 
 def gram(data, factor):
@@ -375,8 +380,8 @@
         in_specs=[pl.BlockSpec(memory_space=pltpu.VMEM)],
         out_specs=pl.BlockSpec(memory_space=pl.ANY),
         scratch_shapes=[
-            pltpu.VMEM((2, 2, 1024, COLUMNS), jnp.float32),
-            pltpu.SemaphoreType.DMA((2,)),
+            pltpu.VMEM((1024 // COLUMNS, 2, 1024, COLUMNS), jnp.float32),
+            pltpu.SemaphoreType.DMA((1024 // COLUMNS,)),
         ],
         compiler_params=pltpu.CompilerParams(vmem_limit_bytes=48 << 20),
         name="gram",

time: 57.6 us -> 56 us (0.972)
  the two profiles are of different devices: /device:TPU:32 before, /device:TPU:64 now
where the time goes in v4:
time: 56 us; the launch traced here: 55.9 us
  Pallas kernels  55.2 us (99%)
  local copies, waits for them, and re-layouts  0.7 us (1%)
    pallas_call x1, Pallas kernels, exchange(): pl.pallas_call(exchange_kernel, out_shape=jax.ShapeDtypeStruct((128, INPU...  50.3 us
    pallas_call x1, Pallas kernels, gram(): pl.pallas_call(functools.partial(gram_kernel, factor), out_shape=jax.Shap...  4.88 us

profile of v4, /device:TPU:64, one launch (start us, length us, event | category | flops | bytes accessed | tf_op | source)
XLA Modules:
  0.0 55.9 jit_solution(2906558861338992093)
XLA Ops:
  0.0 0.0 copy-start
  0.0 0.7 %copy-done = f32[12,32]{1,0:T(8,128)S(1)} copy-done((f32[12,32]{1,0:T(8,128)S(1)}, f32[12,32]{1,0:T(8,128)}, u32[]{:S(2)}) %copy-start) | copy-done | bytes 1560
  0.7 50.3 %exchange.1 = bf16[128,16,384]{2,1,0:T(8,128)(2,1)S(1)} custom-call(bf16[2,8,16,3072]{3,2,1,0:T(8,128)(2,1)} %volts.1, f32[12,32]{1,0:T(8,128)S(1)} %copy-done), custom_call_target="tpu_custom_call" | custom-call | tf_op jit(solution)/shard_map/exchange/pallas_call | solution.py:319
  51.0 4.9 %gram.1 = f32[2,1024,1024]{2,1,0:T(8,128)} custom-call(bf16[2,1024,384]{2,1,0:T(8,128)(2,1)S(1)} %bitcast.2), custom_call_target="tpu_custom_call" | custom-call | tf_op jit(solution)/shard_map/gram/pallas_call | solution.py:377
Async XLA Ops:
  0.0 0.7 %copy-start = (f32[12,32]{1,0:T(8,128)S(1)}, f32[12,32]{1,0:T(8,128)}, u32[]{:S(2)}) copy-start(f32[12,32]{1,0:T(8,128)} %taps.1) | copy-start | bytes 4612

commit v5 on v4

--- a/solution.py
+++ b/solution.py
@@ -77,7 +77,8 @@
     barrier = pltpu.get_barrier_semaphore()
 
     def coarse_at(k):
-        return (zl + k // 2) % 4 * 2 + (y // 2 + k) % 2
+        ahead = jnp.where(zh == 0, k // 2, 4 - k // 2)
+        return (zl + ahead) % 4 * 2 + (y // 2 + k) % 2
 
     def own_load(coarse):
         return pltpu.make_async_copy(

time: 56 us -> 57.6 us (1.029)
  the two profiles are of different devices: /device:TPU:64 before, /device:TPU:32 now
where the time goes in v5:
time: 57.6 us; the launch traced here: 56.6 us
  Pallas kernels  55.9 us (97%)
  local copies, waits for them, and re-layouts  0.7 us (1%)
    pallas_call x1, Pallas kernels, exchange(): pl.pallas_call(exchange_kernel, out_shape=jax.ShapeDtypeStruct((128, INPU...  51.1 us
    pallas_call x1, Pallas kernels, gram(): pl.pallas_call(functools.partial(gram_kernel, factor), out_shape=jax.Shap...  4.88 us

profile of v5, /device:TPU:32, one launch (start us, length us, event | category | flops | bytes accessed | tf_op | source)
XLA Modules:
  0.0 56.6 jit_solution(11287629264415316766)
XLA Ops:
  0.0 0.0 copy-start
  0.0 0.7 %copy-done = f32[12,32]{1,0:T(8,128)S(1)} copy-done((f32[12,32]{1,0:T(8,128)S(1)}, f32[12,32]{1,0:T(8,128)}, u32[]{:S(2)}) %copy-start) | copy-done | bytes 1560
  0.7 51.1 %exchange.1 = bf16[128,16,384]{2,1,0:T(8,128)(2,1)S(1)} custom-call(bf16[2,8,16,3072]{3,2,1,0:T(8,128)(2,1)} %volts.1, f32[12,32]{1,0:T(8,128)S(1)} %copy-done), custom_call_target="tpu_custom_call" | custom-call | tf_op jit(solution)/shard_map/exchange/pallas_call | solution.py:320
  51.8 4.9 %gram.1 = f32[2,1024,1024]{2,1,0:T(8,128)} custom-call(bf16[2,1024,384]{2,1,0:T(8,128)(2,1)S(1)} %bitcast.2), custom_call_target="tpu_custom_call" | custom-call | tf_op jit(solution)/shard_map/gram/pallas_call | solution.py:378
Async XLA Ops:
  0.0 0.7 %copy-start = (f32[12,32]{1,0:T(8,128)S(1)}, f32[12,32]{1,0:T(8,128)}, u32[]{:S(2)}) copy-start(f32[12,32]{1,0:T(8,128)} %taps.1) | copy-start | bytes 4612
